TPU v7x, 32 devices: a whole 2x2x4 slice. The times are simulated.
32 devices in a mesh: groups: 2 (over y), col: 4 (over z), row: 4 (over x, core).
Axes of the slice: x: 2, y: 2, z: 4, core: 2. Of those that a mesh axis runs over, the one named last changes fastest.
Arguments:
- pair_slab: bfloat16 [128, 512, 128], P(('groups', 'row'), 'col'), parts along dimension 0, may hold values from -6 to 6
- tile_pair: bfloat16 [8, 2, 128, 128, 128], P(('groups', 'col'), None, 'row'), parts along dimension 0, may hold values from -6 to 6
- tile_cotan: bfloat16 [8, 2, 128, 128, 128], P(('groups', 'col'), None, 'row'), parts along dimension 0, may hold values from -6 to 6
- tile_rows: int32 [8, 2], P(('groups', 'col')), parts along dimension 0, may hold values from 0 to 3, as said below
- tile_count: int32 [8], P(('groups', 'col')), parts along dimension 0, may hold values from 1 to 2, as said below
- norm_gain: float32 [128], replicated, may hold values from 0.5 to 1.5
- norm_bias: float32 [128], replicated, may hold values from -2.5 to 2.5
- w_in: bfloat16 [128, 512], replicated, may hold values from -0.5 to 0.5
- out_gain: float32 [128], replicated, may hold values from 0.5 to 1.5
- out_bias: float32 [128], replicated, may hold values from -2.5 to 2.5
- w_out: bfloat16 [128, 128], replicated, may hold values from -0.5 to 0.5
- w_gate: bfloat16 [128, 128], replicated, may hold values from -0.5 to 0.5
Outputs:
- update: bfloat16 [8, 2, 128, 128, 128], P(('groups', 'col'), None, 'row'), parts along dimension 0
- grad_slab: bfloat16 [128, 512, 128], P(('groups', 'row'), 'col'), parts along dimension 0
- grad_tiles: bfloat16 [8, 2, 128, 128, 128], P(('groups', 'col'), None, 'row'), parts along dimension 0
- grad_in_w: float32 [256, 512], P('groups'), parts along dimension 0
- grad_out_w: float32 [256, 128], P('groups'), parts along dimension 0
- grad_gate_w: float32 [256, 128], P('groups'), parts along dimension 0
There are 2 independent parts, one for each index of `groups`. A program takes and returns all parts, laid end to end along the dimension named above; an argument that names none is the same for every part. Nothing has to cross between parts.
Inputs may be any that keep to these rules, and one draw needn't show every extreme that they name: `tile_count`: every column block has at least one active slot and some column block has all 2 active. `tile_rows`: the row blocks named by the slots of one column block are distinct; slots at or past the count are inactive.
All inputs are finite; a program needn't handle non-finite values.
Results may differ from a plain program's by a relative error of at most 0.015.
Values may be sent and summed in bfloat16 or wider, within the bound.
A program may use at most 128 MiB of HBM per device.

v0:
```python
import jax
import jax.numpy as jnp
from jax import lax
from jax.sharding import PartitionSpec as P

epsilon = 1e-05


def normalize(values):
    center = values - jnp.mean(values, axis=-1, keepdims=True)
    variance = jnp.mean(center * center, axis=-1, keepdims=True)
    inverse = lax.rsqrt(variance + epsilon)
    return (center * inverse, inverse)


def norm_back(grad_in, centred, inverse, gain):
    scaled = grad_in * gain
    first = jnp.mean(scaled, axis=-1, keepdims=True)
    second = jnp.mean(scaled * centred, axis=-1, keepdims=True)
    return inverse * (scaled - first - centred * second)


def rounded(values):
    return lax.optimization_barrier(values.astype(jnp.bfloat16)).astype(jnp.float32)


def body(
    pair_slab,
    tile_pair,
    tile_cotan,
    tile_rows,
    tile_count,
    norm_gain,
    norm_bias,
    w_in,
    out_gain,
    out_bias,
    w_out,
    w_gate,
):
    k_local, tile_len, channels = pair_slab.shape
    hidden_w = w_out.shape[0]
    slots = tile_rows.shape[1]
    row_count = lax.axis_size("row")
    col_count = lax.axis_size("col")
    row_part = tile_len // row_count
    slab_hat, slab_inv = normalize(pair_slab.astype(jnp.float32))
    slab_norm = (slab_hat * norm_gain + norm_bias).astype(jnp.bfloat16)
    flat_norm = slab_norm.reshape(-1, channels)
    project = jnp.dot(flat_norm, w_in, preferred_element_type=jnp.float32).reshape(
        k_local, tile_len, 4 * hidden_w
    )
    left_proj = project[..., :hidden_w]
    left_sig = jax.nn.sigmoid(project[..., hidden_w : 2 * hidden_w])
    right_proj = project[..., 2 * hidden_w : 3 * hidden_w]
    right_sig = jax.nn.sigmoid(project[..., 3 * hidden_w :])
    left_edges = (left_sig * left_proj).astype(jnp.bfloat16)
    right_edges = (right_sig * right_proj).astype(jnp.bfloat16)
    row_blocks = tile_rows[0]
    active = (jnp.arange(slots) < tile_count[0]).astype(jnp.float32)
    selector = (row_blocks[:, None] == jnp.arange(col_count)[None, :]).astype(jnp.float32) * active[
        :, None
    ]
    spread = lax.all_to_all(
        left_edges.reshape(k_local, row_count, row_part, hidden_w),
        "row",
        split_axis=1,
        concat_axis=0,
        tiled=True,
    )
    panels = lax.all_gather(spread, "col", axis=1, tiled=True)
    chosen = jnp.take(panels, row_blocks, axis=1)
    right_full = lax.all_gather(right_edges, "row", axis=0, tiled=True)
    grouped = jnp.einsum(
        "gksih,gkjh->gsijh",
        chosen.reshape(row_count, k_local, slots, row_part, hidden_w),
        right_full.reshape(row_count, k_local, tile_len, hidden_w),
        preferred_element_type=jnp.float32,
    )
    combined = jnp.sum(rounded(grouped), axis=0)
    comb_hat, comb_inv = normalize(combined)
    comb_norm = (comb_hat * out_gain + out_bias).astype(jnp.bfloat16)
    pair_hat, pair_inv = normalize(tile_pair[0].astype(jnp.float32))
    pair_norm = (pair_hat * norm_gain + norm_bias).astype(jnp.bfloat16)
    flat_comb = comb_norm.reshape(-1, hidden_w)
    flat_pair = pair_norm.reshape(-1, channels)
    mixed = jnp.dot(flat_comb, w_out, preferred_element_type=jnp.float32)
    gate = jax.nn.sigmoid(jnp.dot(flat_pair, w_gate, preferred_element_type=jnp.float32))
    row_mask = jnp.repeat(active, row_part * tile_len)[:, None]
    update = (row_mask * gate * mixed).astype(jnp.bfloat16)
    cotan = tile_cotan[0].astype(jnp.float32).reshape(-1, channels) * row_mask
    grad_mixed = (cotan * gate).astype(jnp.bfloat16)
    grad_logit = (cotan * mixed * gate * (1.0 - gate)).astype(jnp.bfloat16)
    grad_out_w = jnp.dot(flat_comb.T, grad_mixed, preferred_element_type=jnp.float32)
    grad_gate_w = jnp.dot(flat_pair.T, grad_logit, preferred_element_type=jnp.float32)
    out_total, gate_total = (grad_out_w, grad_gate_w)
    grad_comb = jnp.dot(grad_mixed, w_out.T, preferred_element_type=jnp.float32).reshape(
        slots, row_part, tile_len, hidden_w
    )
    grad_pair = jnp.dot(grad_logit, w_gate.T, preferred_element_type=jnp.float32).reshape(
        slots, row_part, tile_len, channels
    )
    pair_back = norm_back(grad_pair, pair_hat, pair_inv, norm_gain).astype(jnp.bfloat16)
    comb_back = norm_back(grad_comb, comb_hat, comb_inv, out_gain).astype(jnp.bfloat16)
    left_term = rounded(
        jnp.einsum("sijh,kjh->ksih", comb_back, right_full, preferred_element_type=jnp.float32)
    )
    routed = jnp.einsum("ksih,sb->kbih", left_term, selector)
    column_sum = lax.psum_scatter(
        routed.astype(jnp.bfloat16), "col", scatter_dimension=1, tiled=True
    ).astype(jnp.float32)
    returned = lax.all_to_all(
        column_sum.reshape(row_count, k_local, row_part, hidden_w).astype(jnp.bfloat16),
        "row",
        split_axis=0,
        concat_axis=2,
        tiled=True,
    ).astype(jnp.float32)
    left_grad = returned.reshape(k_local, tile_len, hidden_w)
    right_part = jnp.einsum(
        "sijh,ksih->skjh", comb_back, chosen, preferred_element_type=jnp.float32
    )
    right_grad = jnp.sum(
        lax.psum_scatter(
            right_part.astype(jnp.bfloat16), "row", scatter_dimension=1, tiled=True
        ).astype(jnp.float32),
        axis=0,
    )
    grad_project = jnp.concatenate(
        [
            left_grad * left_sig,
            left_grad * left_proj * left_sig * (1.0 - left_sig),
            right_grad * right_sig,
            right_grad * right_proj * right_sig * (1.0 - right_sig),
        ],
        axis=-1,
    ).astype(jnp.bfloat16)
    flat_grad = grad_project.reshape(-1, 4 * hidden_w)
    grad_in_w = jnp.dot(flat_norm.T, flat_grad, preferred_element_type=jnp.float32)
    grad_norm = jnp.dot(flat_grad, w_in.T, preferred_element_type=jnp.float32).reshape(
        k_local, tile_len, channels
    )
    grad_slab = norm_back(grad_norm, slab_hat, slab_inv, norm_gain).astype(jnp.bfloat16)
    in_total, out_total, gate_total = lax.psum((grad_in_w, out_total, gate_total), ("col", "row"))
    update_out = update.reshape(1, slots, row_part, tile_len, channels)
    tiles_out = pair_back.reshape(1, slots, row_part, tile_len, channels)
    return (update_out, grad_slab, tiles_out, in_total, out_total, gate_total)


def solution(mesh):
    return jax.shard_map(
        body,
        mesh=mesh,
        in_specs=(
            P(("groups", "row"), "col", None),
            P(("groups", "col"), None, "row", None, None),
            P(("groups", "col"), None, "row", None, None),
            P(("groups", "col"), None),
            P(("groups", "col")),
            P(),
            P(),
            P(),
            P(),
            P(),
            P(),
            P(),
        ),
        out_specs=(
            P(("groups", "col"), None, "row", None, None),
            P(("groups", "row"), "col", None),
            P(("groups", "col"), None, "row", None, None),
            P("groups", None),
            P("groups", None),
            P("groups", None),
        ),
        check_vma=False,
    )
```

profile of v0, /device:TPU:0, one launch (start us, length us, event | category | flops | bytes accessed | tf_op | source)
XLA Modules:
  0.0 364.9 jit_solution(873537648331085904)
XLA Ops:
  14.5 4.2 %all-to-all-start = ((bf16[16,4,32,128]{3,2,0,1:T(8,128)(2,1)}), bf16[16,4,32,128]{3,2,0,1:T(8,128)(2,1)S(1)}, u32[]{:S(2)}, u32[]{:S(2)}) async-start(bf16[16,4,32,128]{3,2,0,1:T(8,128)(2,1)} %copy.57), calls=%async_computation | async-start | bytes 1048576 | tf_op jit(solution)/shard_map/all_to_all | solution.py:64
  19.5 9.8 %all-to-all-done = bf16[16,4,32,128]{3,2,0,1:T(8,128)(2,1)S(1)} async-done(((bf16[16,4,32,128]{3,2,0,1:T(8,128)(2,1)}), bf16[16,4,32,128]{3,2,0,1:T(8,128)(2,1)S(1)}, u32[]{:S(2)}, u32[]{:S(2)}) %all-to-all-start) | async-done | bytes 524320 | tf_op jit(solution)/shard_map/all_to_all | solution.py:64
  40.3 4.5 %copy.74 = bf16[4,16,128,128,1]{2,1,4,3,0:T(8,128)(2,1)} copy(bf16[4,16,128,128,1]{3,2,1,0,4:T(8,128)(2,1)} %bitcast.112) | data formatting | bytes 4194304 | tf_op jit(solution)/shard_map/reshape | solution.py:77
  44.8 4.2 %copy.75 = bf16[64,128,128,1]{1,0,3,2:T(8,128)(2,1)} copy(bf16[64,128,128,1]{2,1,0,3:T(8,128)(2,1)} %bitcast.113) | data formatting | bytes 4194304 | tf_op jit(solution)/shard_map/all_gather | solution.py:73
  49.0 40.4 %all-gather.5.cloned.1.call-done = bf16[64,4,32,128]{3,2,1,0:T(8,128)(2,1)} async-done(((bf16[64,1,32,128]{3,2,1,0:T(8,128)(2,1)}), bf16[64,4,32,128]{3,2,1,0:T(8,128)(2,1)}) %all-gather.5.cloned.1.call-update) | async-done | bytes 2097168 | tf_op jit(solution)/shard_map/all_gather | solution.py:71
  95.2 7.2 %copy.61 = bf16[4,16,2,32,128]{3,1,2,4,0:T(8,128)(2,1)} copy(bf16[4,16,2,32,128]{4,3,2,1,0:T(8,128)(2,1)} %broadcast_select_fusion.1) | data formatting | bytes 2097152 | tf_op jit(solution)/shard_map/jit(_take)/select_n | solution.py:72
  102.4 5.2 %convert_bitcast_fusion = bf16[4,2,32,128,128]{3,2,1,4,0:T(8,128)(2,1)S(1)} fusion(bf16[4,16,128,128,1]{2,1,4,3,0:T(8,128)(2,1)} %copy.74, bf16[4,16,2,32,128]{3,1,2,4,0:T(8,128)(2,1)} %copy.61), kind=kOutput, calls=%fused_computation.7 | convolution fusion | flops 138412032 | bytes 11534336 | tf_op jit(solution)/shard_map/gksih,gkjh->gsijh/dot_general | solution.py:74
  107.7 5.1 %convert_reduce_fusion = (f32[2,32,128]{2,1,0:T(8,128)S(1)}, f32[2,32,128,128]{2,1,0,3:T(8,128)}) fusion(bf16[4,2,32,128,128]{3,2,1,4,0:T(8,128)(2,1)S(1)} %convert_bitcast_fusion), kind=kLoop, calls=%fused_computation.1 | loop fusion | flops 11526144 | bytes 12615680 | tf_op jit(solution)/shard_map/reduce_sum | solution.py:10
  112.7 5.3 %copy.62 = f32[2,32,128,128]{3,2,1,0:T(8,128)} copy(f32[2,32,128,128]{2,1,0,3:T(8,128)} %get-tuple-element.31) | data formatting | bytes 8388608 | tf_op jit(solution)/shard_map/reduce_sum | solution.py:80
  121.5 4.5 %add_convert_fusion = bf16[8192,128]{1,0:T(8,128)(2,1)S(1)} fusion(f32[2,32,128,128]{3,2,1,0:T(8,128)S(1)} %copy-done.2, f32[128]{0:T(128)S(1)} %copy-done.18, f32[128]{0:T(128)S(1)} %copy-done.15, f32[8192]{0:T(1024)S(1)} %bitcast.123, f32[8192]{0:T(1024)S(1)} %bitcast.119), kind=kLoop, calls=%fused_computation.28 | loop fusion | flops 5242880 | bytes 6358016 | tf_op jit(solution)/shard_map/convert_element_type | solution.py:82
  129.1 4.3 %fusion.8 = (bf16[8192,128]{1,0:T(8,128)(2,1)}, bf16[8192,128]{1,0:T(8,128)(2,1)}, bf16[8192,128]{1,0:T(8,128)(2,1)S(1)}) fusion(f32[8192,128]{1,0:T(8,128)S(1)} %fusion.48, bf16[1,2,32,128,128]{4,3,2,1,0:T(8,128)(2,1)S(1)} %copy-done.19, f32[8192]{0:T(1024)S(1)} %bitcast.132, bf16[8192,128]{1,0:T(8,128)(2,1)S(1)} %copy-done.7, ...), kind=kOutput, calls=%fused_computation.14 | convolution fusion | flops 284164096 | bytes 14745600 | tf_op jit(solution)/shard_map/dot_general | solution.py:88
  133.4 6.2 %multiply_reduce_fusion.4 = (f32[8192]{0:T(1024)S(1)}, f32[8192]{0:T(1024)S(1)}, f32[8192,128]{1,0:T(8,128)}) fusion(f32[128]{0:T(128)S(1)} %copy-done.15, f32[8192]{0:T(1024)S(1)} %bitcast.124, f32[8192]{0:T(1024)S(1)} %bitcast.120, f32[2,32,128,128]{3,2,1,0:T(8,128)S(1)} %copy-done.2, bf16[8192,128]{1,0:T(8,128)(2,1)S(1)} %get-tuple-element.43, ...), kind=kOutput, calls=%fused_computation.32 | convolution fusion | flops 274710528 | bytes 10650112 | tf_op jit(solution)/shard_map/dot_general | solution.py:97
  139.6 5.5 %copy.63 = f32[2,32,128,128]{2,1,0,3:T(8,128)} copy(f32[2,32,128,128]{3,2,1,0:T(8,128)} %bitcast.110) | data formatting | bytes 8388608 | tf_op jit(solution)/shard_map/reshape | solution.py:97
  145.1 4.8 %multiply_convert_fusion.1 = bf16[2,32,128,128]{2,1,0,3:T(8,128)(2,1)S(1)} fusion(f32[2,32,128,128]{2,1,0,3:T(8,128)} %copy.63, f32[2,32,128,128]{2,1,0,3:T(8,128)} %get-tuple-element.31, f32[2,32,128]{2,1,0:T(8,128)S(1)} %bitcast.128, f32[2,32,128]{2,1,0:T(8,128)S(1)} %bitcast.129, f32[128]{0:T(128)S(1)} %copy-done.15, f32[2,32,128]{2,1,0:T(8,128)S(1)} %add_rsqrt_fusion, ...), kind=kLoop, calls=%fused_computation.25 | loop fusion | flops 8388608 | bytes 10617344 | tf_op jit(solution)/shard_map/convert_element_type | solution.py:104
  153.8 4.7 %copy.65 = bf16[64,2,32,128]{3,1,2,0:T(2,128)(2,1)} copy(bf16[64,2,32,128]{0,2,1,3:T(8,128)(2,1)} %convert_bitcast_fusion.3) | data formatting | bytes 2097152 | tf_op jit(solution)/shard_map/optimization_barrier | solution.py:24
  165.4 5.4 %copy.68 = bf16[64,2,32,128]{0,2,3,1:T(8,128)(2,1)} copy(bf16[64,2,32,128]{3,2,0,1:T(8,128)(2,1)} %broadcast_select_fusion) | data formatting | bytes 2097152 | tf_op jit(solution)/shard_map/jit(_take)/select_n | solution.py:72
  170.8 5.5 %convert_bitcast_fusion.1 = bf16[2,64,128,128]{2,1,3,0:T(8,128)(2,1)} fusion(bf16[64,2,32,128]{0,2,3,1:T(8,128)(2,1)} %copy.68, bf16[2,32,128,128]{2,1,0,3:T(8,128)(2,1)} %copy-done.5), kind=kOutput, calls=%fused_computation.24 | convolution fusion | flops 136314880 | bytes 7340032 | tf_op jit(solution)/shard_map/sijh,ksih->skjh/dot_general | solution.py:120
  176.3 7.2 %multiply_reduce_fusion.3 = (f32[8192]{0:T(1024)S(1)}, f32[8192]{0:T(1024)S(1)}, f32[8192,128]{1,0:T(8,128)S(1)}) fusion(f32[128]{0:T(128)S(1)} %copy-done.16, f32[8192]{0:T(1024)S(1)} %bitcast.127, f32[8192]{0:T(1024)S(1)} %bitcast.122, bf16[1,2,32,128,128]{4,3,2,1,0:T(8,128)(2,1)S(1)} %copy-done.3, bf16[8192,128]{1,0:T(8,128)(2,1)} %get-tuple-element.41, ...), kind=kOutput, calls=%fused_computation.31 | convolution fusion | flops 275759104 | bytes 8552960 | tf_op jit(solution)/shard_map/dot_general | solution.py:100
  183.5 5.9 %multiply_convert_fusion = bf16[1,2,32,128,128]{4,3,2,1,0:T(8,128)(2,1)} fusion(f32[1,2,32,128,128]{4,3,2,1,0:T(8,128)S(1)} %bitcast.115, bf16[1,2,32,128,128]{4,3,2,1,0:T(8,128)(2,1)S(1)} %copy-done.3, f32[2,32,128]{2,1,0:T(8,128)S(1)} %bitcast.130, f32[2,32,128]{2,1,0:T(8,128)S(1)} %broadcast_multiply_fusion.5, f32[2,32,128]{2,1,0:T(8,128)S(1)} %bitcast.131, ...), kind=kLoop, calls=%fused_computation.22 | loop fusion | flops 9437184 | bytes 8520192 | tf_op jit(solution)/shard_map/convert_element_type | solution.py:103
  189.4 16.3 %reduce-scatter.3.cloned.1.call-done = bf16[64,1,32,128]{3,2,0,1:T(8,128)(2,1)} async-done(((bf16[64,4,32,128]{3,2,0,1:T(8,128)(2,1)}), bf16[64,1,32,128]{3,2,0,1:T(8,128)(2,1)}) %reduce-scatter.3.cloned.1.call-update) | async-done | bytes 524304 | tf_op jit(solution)/shard_map/reduce_scatter | solution.py:109
  209.6 3.8 %fusion.49 = f32[128,128]{1,0:T(8,128)} fusion(bf16[8192,128]{1,0:T(8,128)(2,1)} %copy-done.4, bf16[8192,128]{1,0:T(8,128)(2,1)} %copy-done.9), kind=kOutput, calls=%fused_computation.105 | convolution fusion | flops 268435456 | bytes 4259840 | tf_op jit(solution)/shard_map/dot_general | solution.py:94
  218.3 33.9 %reduce-scatter.5.cloned.1.call-done = bf16[2,16,128,128]{2,1,3,0:T(8,128)(2,1)} async-done(((bf16[2,64,128,128]{2,1,3,0:T(8,128)(2,1)}), bf16[2,16,128,128]{2,1,3,0:T(8,128)(2,1)}) %reduce-scatter.5.cloned.1.call-update) | async-done | bytes 1048592 | tf_op jit(solution)/shard_map/reduce_scatter | solution.py:124
  255.0 3.6 multiply_convert_fusion.6
  264.0 89.7 %all-reduce.3.cloned.1.call-done = (f32[128,512]{1,0:T(8,128)}, f32[128,128]{1,0:T(8,128)}, f32[128,128]{1,0:T(8,128)}) async-done(((f32[128,512]{1,0:T(8,128)}, f32[128,128]{1,0:T(8,128)}, f32[128,128]{1,0:T(8,128)}), (f32[128,512]{1,0:T(8,128)}, f32[128,128]{1,0:T(8,128)}, f32[128,128]{1,0:T(8,128)})) %all-reduce.3.cloned.1.call-update) | async-done | bytes 393232 | tf_op jit(solution)/shard_map/psum | solution.py:144
  (103 shorter events, 62.9 us)
Async XLA Ops:
  7.2 33.2 %all-gather.3.cloned.1.call-start = ((), (), s32[]{:S(2)}) async-start(), calls=%async_computation.4 | async-start | bytes 2621440 | tf_op jit(solution)/shard_map/all_gather | solution.py:73
  10.4 1.9 copy-start.1
  12.3 7.2 %copy-start.21 = (s32[1,2]{1,0:T(1,128)S(1)}, s32[1,2]{1,0:T(1,128)}, u32[]{:S(2)}) copy-start(s32[1,2]{1,0:T(1,128)} %param.15) | copy-start | bytes 28
  12.3 17.9 %copy-start.3 = (bf16[1,2,32,128,128]{4,3,2,1,0:T(8,128)(2,1)S(1)}, bf16[1,2,32,128,128]{4,3,2,1,0:T(8,128)(2,1)}, u32[]{:S(2)}) copy-start(bf16[1,2,32,128,128]{4,3,2,1,0:T(8,128)(2,1)} %param.13) | copy-start | bytes 6291460
  13.7 19.8 %copy-start.16 = (f32[128]{0:T(128)S(1)}, f32[128]{0:T(128)}, u32[]{:S(2)}) copy-start(f32[128]{0:T(128)} %param.17) | copy-start | bytes 1540
  13.7 19.8 %copy-start.17 = (f32[128]{0:T(128)S(1)}, f32[128]{0:T(128)}, u32[]{:S(2)}) copy-start(f32[128]{0:T(128)} %param.18) | copy-start | bytes 1540
  14.5 14.8 %all-to-all-start = ((bf16[16,4,32,128]{3,2,0,1:T(8,128)(2,1)}), bf16[16,4,32,128]{3,2,0,1:T(8,128)(2,1)S(1)}, u32[]{:S(2)}, u32[]{:S(2)}) async-start(bf16[16,4,32,128]{3,2,0,1:T(8,128)(2,1)} %copy.57), calls=%async_computation | async-start | bytes 1048576 | tf_op jit(solution)/shard_map/all_to_all | solution.py:64
  18.7 70.7 %all-gather.5.cloned.1.call-start = ((), (), s32[]{:S(2)}) async-start(), calls=%async_computation.5 | async-start | bytes 2621440 | tf_op jit(solution)/shard_map/all_gather | solution.py:71
  30.1 175.6 %reduce-scatter.3.cloned.1.call-start = ((), (), s32[]{:S(2)}) async-start(), calls=%async_computation.6 | async-start | bytes 2621440 | tf_op jit(solution)/shard_map/reduce_scatter | solution.py:109
  118.1 3.4 copy-start.2
  118.1 3.4 copy-start.15
  118.1 3.5 copy-start.18
  120.9 5.2 %copy-start.14 = (bf16[128,128]{1,0:T(8,128)(2,1)S(1)}, bf16[128,128]{1,0:T(8,128)(2,1)}, u32[]{:S(2)}) copy-start(bf16[128,128]{1,0:T(8,128)(2,1)} %param.22) | copy-start | bytes 98308
  126.1 2.3 copy-start.7
  126.1 3.0 copy-start.19
  126.1 3.0 copy-start.20
  133.4 6.2 %copy-start.9 = (bf16[8192,128]{1,0:T(8,128)(2,1)}, bf16[8192,128]{1,0:T(8,128)(2,1)S(1)}, u32[]{:S(2)}) copy-start(bf16[8192,128]{1,0:T(8,128)(2,1)S(1)} %get-tuple-element.43) | copy-start | bytes 6291460
  145.1 6.2 %copy-start.6 = (bf16[64,128,128,1]{1,0,3,2:T(8,128)(2,1)S(1)}, bf16[64,128,128,1]{1,0,3,2:T(8,128)(2,1)}, u32[]{:S(2)}) copy-start(bf16[64,128,128,1]{1,0,3,2:T(8,128)(2,1)} %copy.75) | copy-start | bytes 6291460
  163.0 89.1 %reduce-scatter.5.cloned.1.call-start = ((), (), s32[]{:S(2)}) async-start(), calls=%async_computation.7 | async-start | bytes 5242880 | tf_op jit(solution)/shard_map/reduce_scatter | solution.py:124
  189.4 23.9 %copy-start.8 = (bf16[8192,128]{1,0:T(8,128)(2,1)S(1)}, bf16[8192,128]{1,0:T(8,128)(2,1)}, u32[]{:S(2)}) copy-start(bf16[8192,128]{1,0:T(8,128)(2,1)} %add_convert_fusion.1) | copy-start | bytes 6291460
  205.8 12.3 %all-to-all-start.1 = ((bf16[4,16,32,128]{3,2,1,0:T(8,128)(2,1)}), bf16[4,16,32,128]{3,2,1,0:T(8,128)(2,1)S(1)}, u32[]{:S(2)}, u32[]{:S(2)}) async-start(bf16[4,16,32,128]{3,2,1,0:T(8,128)(2,1)} %bitcast.125), calls=%async_computation.2 | async-start | bytes 1048576 | tf_op jit(solution)/shard_map/all_to_all | solution.py:112
  209.2 144.5 %all-reduce.3.cloned.1.call-start = ((), (), s32[]{:S(2)}) async-start(), calls=%async_computation.8 | async-start | bytes 786432 | tf_op jit(solution)/shard_map/psum | solution.py:144
  209.5 3.8 %copy-start.10 = (bf16[8192,128]{1,0:T(8,128)(2,1)S(1)}, bf16[8192,128]{1,0:T(8,128)(2,1)}, u32[]{:S(2)}) copy-start(bf16[8192,128]{1,0:T(8,128)(2,1)} %get-tuple-element.41) | copy-start | bytes 6291460
  258.7 2.0 copy-start.12
  (5 other events, 6.0 us)
Sparse Core Ops, SparseCore 0:
  13.8 26.4 all-gather.2
  42.5 46.9 all-gather.4
  163.1 42.5 reduce-scatter.2
  208.3 43.8 reduce-scatter.4
  262.8 90.8 all-reduce.2
where the time goes:
time: 366 us; the launch traced here: 365 us
  waiting for transfers between devices  197 us (54%)
  local copies, waits for them, and re-layouts  60.2 us (16%)
  matrix products  44.3 us (12%)
  other arithmetic  40.4 us (11%)
  between operations  14.8 us (4%)
  starting transfers between devices  8.1 us (2%)
    psum x1, waiting for transfers between devices, body(): lax.psum((grad_in_w, out_total, gate_total), ('col', 'row'))  89.7 us
    all_gather x1, waiting for transfers between devices, body(): panels = lax.all_gather(spread, 'col', axis=1, tiled=True)  40.4 us
    reduce_scatter x1, waiting for transfers between devices, body(): lax.psum_scatter(right_part.astype(jnp.bfloat16), 'row', scatter_dimensio...  33.9 us
    reduce_scatter x1, waiting for transfers between devices, body(): lax.psum_scatter(routed.astype(jnp.bfloat16), 'col', scatter_dimension=1,...  16.3 us
    unnamed x51, local copies, waits for them, and re-layouts  14.8 us
    select_n x2, local copies, waits for them, and re-layouts, body(): chosen = jnp.take(panels, row_blocks, axis=1)  12.6 us
    all_to_all x1, waiting for transfers between devices, body(): lax.all_to_all(left_edges.reshape(k_local, row_count, row_part, hidden_w)...  9.82 us
  transfers between devices with their start and end apart: 7, of which 7 were waited for; matrix products, arithmetic and copies ran while one was open for 14% of the time, Pallas kernels for 0%

commit v1 on v0

v1 whole, which is shorter than its diff:
```python
import functools

import jax
import jax.numpy as jnp
from jax import lax
from jax.experimental import pallas as pl
from jax.experimental.pallas import tpu as pltpu
from jax.sharding import PartitionSpec as P

epsilon = 1e-05


def normalize(values):
    center = values - jnp.mean(values, axis=-1, keepdims=True)
    variance = jnp.mean(center * center, axis=-1, keepdims=True)
    inverse = lax.rsqrt(variance + epsilon)
    return (center * inverse, inverse)


def norm_back(grad_in, centred, inverse, gain):
    scaled = grad_in * gain
    first = jnp.mean(scaled, axis=-1, keepdims=True)
    second = jnp.mean(scaled * centred, axis=-1, keepdims=True)
    return inverse * (scaled - first - centred * second)


def dot(left, right, left_dim, right_dim):
    return lax.dot_general(
        left,
        right,
        (((left_dim,), (right_dim,)), ((), ())),
        preferred_element_type=jnp.float32,
    )


def to_hidden_major(values):
    return jnp.swapaxes(jnp.swapaxes(values, 1, 2), 0, 1)


def from_hidden_major(values):
    return jnp.swapaxes(jnp.swapaxes(values, 0, 1), 1, 2)


def tile_kernel(
    rows_ref,
    count_ref,
    panels_ref,
    right_ref,
    pair_ref,
    cotan_ref,
    norm_gain_ref,
    norm_bias_ref,
    out_gain_ref,
    out_bias_ref,
    w_out_ref,
    w_gate_ref,
    update_ref,
    tiles_ref,
    left_ref,
    right_part_ref,
    out_w_ref,
    gate_w_ref,
    left_major,
    right_major,
    comb_major,
    back_major,
    right_back,
    left_back,
):
    depth, tile_len, hidden = right_ref.shape
    slots, row_part, _, channels = pair_ref.shape
    chunk = 16
    norm_gain, norm_bias = norm_gain_ref[...], norm_bias_ref[...]
    out_gain, out_bias = out_gain_ref[...], out_bias_ref[...]

    @pl.loop(0, depth // chunk)
    def _(step):
        at = pl.ds(pl.multiple_of(step * chunk, chunk), chunk)
        block = right_ref[at].astype(jnp.float32)
        right_major[:, at, :] = to_hidden_major(block).astype(jnp.bfloat16)
        parts = [panels_ref[rows_ref[0, s], at] for s in range(slots)]
        block = jnp.concatenate(parts, axis=1).astype(jnp.float32)
        left_major[:, at, :] = to_hidden_major(block).astype(jnp.bfloat16)
        for column in range(left_ref.shape[0]):
            left_ref[column, at] = jnp.zeros((chunk,) + left_ref.shape[2:], left_ref.dtype)

    @pl.loop(0, hidden, unroll=4)
    def _(h):
        comb_major[h] = dot(left_major[h], right_major[h], 0, 0)

    out_w_ref[...] = jnp.zeros_like(out_w_ref)
    gate_w_ref[...] = jnp.zeros_like(gate_w_ref)
    for s in range(slots):
        active = jnp.where(s < count_ref[0], 1.0, 0.0).astype(jnp.float32)

        @pl.loop(0, row_part // chunk)
        def _(step):
            at = pl.ds(pl.multiple_of(step * chunk, chunk), chunk)
            at_all = pl.ds(pl.multiple_of(s * row_part + step * chunk, chunk), chunk)
            combined = from_hidden_major(comb_major[:, at_all, :]).reshape(-1, hidden)
            comb_hat, comb_inv = normalize(combined)
            comb_norm = (comb_hat * out_gain + out_bias).astype(jnp.bfloat16)
            pair = pair_ref[s, at].astype(jnp.float32).reshape(-1, channels)
            pair_hat, pair_inv = normalize(pair)
            pair_norm = (pair_hat * norm_gain + norm_bias).astype(jnp.bfloat16)
            mixed = dot(comb_norm, w_out_ref[...], 1, 0)
            gate = jax.nn.sigmoid(dot(pair_norm, w_gate_ref[...], 1, 0))
            update = (active * gate * mixed).astype(jnp.bfloat16)
            update_ref[s, at] = update.reshape(chunk, tile_len, channels)
            cotan = cotan_ref[s, at].astype(jnp.float32).reshape(-1, channels) * active
            grad_mixed = (cotan * gate).astype(jnp.bfloat16)
            grad_logit = (cotan * mixed * gate * (1.0 - gate)).astype(jnp.bfloat16)
            out_w_ref[...] += dot(comb_norm, grad_mixed, 0, 0)
            gate_w_ref[...] += dot(pair_norm, grad_logit, 0, 0)
            grad_pair = dot(grad_logit, w_gate_ref[...], 1, 1)
            pair_back = norm_back(grad_pair, pair_hat, pair_inv, norm_gain)
            tiles_ref[s, at] = pair_back.astype(jnp.bfloat16).reshape(chunk, tile_len, channels)
            grad_comb = dot(grad_mixed, w_out_ref[...], 1, 1)
            comb_back = norm_back(grad_comb, comb_hat, comb_inv, out_gain)
            comb_back = comb_back.reshape(chunk, tile_len, hidden)
            back_major[:, at_all, :] = to_hidden_major(comb_back).astype(jnp.bfloat16)

    @pl.loop(0, hidden, unroll=4)
    def _(h):
        back = back_major[h]
        right_back[h] = dot(left_major[h], back, 1, 0).astype(jnp.bfloat16)
        left_back[h] = dot(right_major[h], back, 1, 1).astype(jnp.bfloat16)

    @pl.loop(0, depth // chunk)
    def _(step):
        at = pl.ds(pl.multiple_of(step * chunk, chunk), chunk)
        right_part_ref[at] = from_hidden_major(
            right_back[:, at, :].astype(jnp.float32)
        ).astype(jnp.bfloat16)
        terms = from_hidden_major(left_back[:, at, :].astype(jnp.float32)).astype(jnp.bfloat16)
        for s in range(slots):
            row = rows_ref[0, s]
            left_ref[row, at] += terms[:, s * row_part : (s + 1) * row_part]


def tile_work(rows, count, panels, right_full, pair, cotan, gains, w_out, w_gate):
    depth, tile_len, hidden = right_full.shape
    slots, row_part, _, channels = pair.shape
    cells = slots * row_part
    smem = pl.BlockSpec(memory_space=pltpu.SMEM)
    vmem = pl.BlockSpec(memory_space=pltpu.VMEM)
    half, full = jnp.bfloat16, jnp.float32
    return pl.pallas_call(
        tile_kernel,
        out_shape=(
            jax.ShapeDtypeStruct(pair.shape, half),
            jax.ShapeDtypeStruct(pair.shape, half),
            jax.ShapeDtypeStruct(panels.shape, half),
            jax.ShapeDtypeStruct(right_full.shape, half),
            jax.ShapeDtypeStruct((hidden, channels), full),
            jax.ShapeDtypeStruct((channels, channels), full),
        ),
        in_specs=[smem, smem] + [vmem] * 10,
        out_specs=(vmem,) * 6,
        scratch_shapes=[
            pltpu.VMEM((hidden, depth, cells), half),
            pltpu.VMEM((hidden, depth, tile_len), half),
            pltpu.VMEM((hidden, cells, tile_len), full),
            pltpu.VMEM((hidden, cells, tile_len), half),
            pltpu.VMEM((hidden, depth, tile_len), half),
            pltpu.VMEM((hidden, depth, cells), half),
        ],
        compiler_params=pltpu.CompilerParams(vmem_limit_bytes=58 * 2**20),
        name="tile_work",
    )(rows, count, panels, right_full, pair, cotan, *gains, w_out, w_gate)


def sum_kernel(col_count, row_count, grads_ref, total_ref, outgoing, arrived, summed, sems):
    count, rows, _ = grads_ref.shape
    group = lax.axis_index("groups")
    me = lax.axis_index("col") * row_count + lax.axis_index("row")

    def place(index):
        return (group, index // row_count, index % row_count)

    def piece(step):
        to = (me + step) % count
        return pltpu.make_async_remote_copy(
            src_ref=outgoing.at[step],
            dst_ref=arrived.at[step],
            send_sem=sems.at[0, step],
            recv_sem=sems.at[1, step],
            device_id=place(to),
            device_id_type=pl.DeviceIdType.MESH,
        )

    def share(step):
        to = (me + step) % count
        return pltpu.make_async_remote_copy(
            src_ref=summed.at[0],
            dst_ref=summed.at[step],
            send_sem=sems.at[2, step],
            recv_sem=sems.at[3, step],
            device_id=place(to),
            device_id_type=pl.DeviceIdType.MESH,
        )

    barrier = pltpu.get_barrier_semaphore()

    @pl.loop(1, count)
    def _(step):
        pl.semaphore_signal(
            barrier,
            inc=1,
            device_id=place((me + step) % count),
            device_id_type=pl.DeviceIdType.MESH,
        )

    @pl.loop(1, count)
    def _(step):
        outgoing[step] = grads_ref[(me + step) % count].astype(jnp.bfloat16)

    pl.semaphore_wait(barrier, count - 1)

    @pl.loop(1, count)
    def _(step):
        piece(step).start()

    @pl.loop(1, count)
    def _(step):
        piece(step).wait()

    total = grads_ref[me]
    for step in range(1, count):
        total = total + arrived[step].astype(jnp.float32)
    summed[0] = total.astype(jnp.bfloat16)

    @pl.loop(1, count)
    def _(step):
        share(step).start()

    @pl.loop(1, count)
    def _(step):
        share(step).wait()

    @pl.loop(0, count)
    def _(step):
        total_ref[(me + count - step) % count] = summed[step].astype(jnp.float32)


def sum_over_devices(grads, col_count, row_count):
    count, rows, lanes = grads.shape
    vmem = pl.BlockSpec(memory_space=pltpu.VMEM)
    return pl.pallas_call(
        functools.partial(sum_kernel, col_count, row_count),
        out_shape=jax.ShapeDtypeStruct(grads.shape, grads.dtype),
        in_specs=[vmem],
        out_specs=vmem,
        scratch_shapes=[
            pltpu.VMEM((count, rows, lanes), jnp.bfloat16),
            pltpu.VMEM((count, rows, lanes), jnp.bfloat16),
            pltpu.VMEM((count, rows, lanes), jnp.bfloat16),
            pltpu.SemaphoreType.DMA((4, count)),
        ],
        compiler_params=pltpu.CompilerParams(collective_id=0, has_side_effects=True),
        name="sum_over_devices",
    )(grads)


def body(
    pair_slab,
    tile_pair,
    tile_cotan,
    tile_rows,
    tile_count,
    norm_gain,
    norm_bias,
    w_in,
    out_gain,
    out_bias,
    w_out,
    w_gate,
):
    k_local, tile_len, channels = pair_slab.shape
    hidden_w = w_out.shape[0]
    slots = tile_rows.shape[1]
    row_count = lax.axis_size("row")
    col_count = lax.axis_size("col")
    row_part = tile_len // row_count
    slab_hat, slab_inv = normalize(pair_slab.astype(jnp.float32))
    slab_norm = (slab_hat * norm_gain + norm_bias).astype(jnp.bfloat16)
    flat_norm = slab_norm.reshape(-1, channels)
    project = jnp.dot(flat_norm, w_in, preferred_element_type=jnp.float32).reshape(
        k_local, tile_len, 4 * hidden_w
    )
    left_proj = project[..., :hidden_w]
    left_sig = jax.nn.sigmoid(project[..., hidden_w : 2 * hidden_w])
    right_proj = project[..., 2 * hidden_w : 3 * hidden_w]
    right_sig = jax.nn.sigmoid(project[..., 3 * hidden_w :])
    left_edges = (left_sig * left_proj).astype(jnp.bfloat16)
    right_edges = (right_sig * right_proj).astype(jnp.bfloat16)
    spread = lax.all_to_all(
        left_edges.reshape(k_local, row_count, row_part, hidden_w),
        "row",
        split_axis=1,
        concat_axis=0,
        tiled=True,
    )
    panels = lax.all_gather(spread, "col")
    right_full = lax.all_gather(right_edges, "row", axis=0, tiled=True)
    update, pair_back, routed, right_part, out_total, gate_total = tile_work(
        tile_rows,
        tile_count,
        panels.reshape(col_count, -1, row_part, hidden_w),
        right_full,
        tile_pair[0],
        tile_cotan[0],
        tuple(v[None, :] for v in (norm_gain, norm_bias, out_gain, out_bias)),
        w_out,
        w_gate,
    )
    column_sum = lax.psum_scatter(
        routed, "col", scatter_dimension=0, tiled=True
    ).astype(jnp.float32)
    returned = lax.all_to_all(
        column_sum.reshape(row_count, k_local, row_part, hidden_w).astype(jnp.bfloat16),
        "row",
        split_axis=0,
        concat_axis=2,
        tiled=True,
    ).astype(jnp.float32)
    left_grad = returned.reshape(k_local, tile_len, hidden_w)
    right_grad = lax.psum_scatter(
        right_part, "row", scatter_dimension=0, tiled=True
    ).astype(jnp.float32)
    grad_project = jnp.concatenate(
        [
            left_grad * left_sig,
            left_grad * left_proj * left_sig * (1.0 - left_sig),
            right_grad * right_sig,
            right_grad * right_proj * right_sig * (1.0 - right_sig),
        ],
        axis=-1,
    ).astype(jnp.bfloat16)
    flat_grad = grad_project.reshape(-1, 4 * hidden_w)
    grad_in_w = jnp.dot(flat_norm.T, flat_grad, preferred_element_type=jnp.float32)
    grad_norm = jnp.dot(flat_grad, w_in.T, preferred_element_type=jnp.float32).reshape(
        k_local, tile_len, channels
    )
    grad_slab = norm_back(grad_norm, slab_hat, slab_inv, norm_gain).astype(jnp.bfloat16)
    devices = row_count * col_count
    lanes = 128
    grads = [v.reshape(-1, lanes) for v in (grad_in_w, out_total, gate_total)]
    sizes = [v.shape[0] for v in grads]
    rows = -(-sum(sizes) // (16 * devices)) * 16
    spare = rows * devices - sum(sizes)
    grads = jnp.concatenate(grads + [jnp.zeros((spare, lanes), jnp.float32)] * (spare > 0))
    summed = sum_over_devices(grads.reshape(devices, rows, lanes), col_count, row_count)
    summed = summed.reshape(-1, lanes)
    in_total = summed[: sizes[0]].reshape(grad_in_w.shape)
    out_total = summed[sizes[0] : sizes[0] + sizes[1]].reshape(out_total.shape)
    gate_total = summed[sizes[0] + sizes[1] : sum(sizes)].reshape(gate_total.shape)
    update_out = update.reshape(1, slots, row_part, tile_len, channels)
    tiles_out = pair_back.reshape(1, slots, row_part, tile_len, channels)
    return (update_out, grad_slab, tiles_out, in_total, out_total, gate_total)


def solution(mesh):
    return jax.shard_map(
        body,
        mesh=mesh,
        in_specs=(
            P(("groups", "row"), "col", None),
            P(("groups", "col"), None, "row", None, None),
            P(("groups", "col"), None, "row", None, None),
            P(("groups", "col"), None),
            P(("groups", "col")),
            P(),
            P(),
            P(),
            P(),
            P(),
            P(),
            P(),
        ),
        out_specs=(
            P(("groups", "col"), None, "row", None, None),
            P(("groups", "row"), "col", None),
            P(("groups", "col"), None, "row", None, None),
            P("groups", None),
            P("groups", None),
            P("groups", None),
        ),
        check_vma=False,
    )
```

time: 366 us -> 235 us (0.64)
  waiting for transfers between devices: 197 us -> 123 us
  Pallas kernels: 0 us -> 56.3 us
  local copies, waits for them, and re-layouts: 60.2 us -> 6.14 us
  matrix products: 44.3 us -> 2.15 us
  other arithmetic: 40.4 us -> 6.64 us
  blocking collectives: 0 us -> 25.6 us
  starting transfers between devices: 8.1 us -> 0.16 us
    psum x1 -> x0, waiting for transfers between devices: 89.7 us -> none  [body(): lax.psum((grad_in_w, out_total, gate_total), ('col', 'row'))]
    pallas_call x0 -> x2, Pallas kernels: none -> 56.3 us  [the longest x1 39.6 us: tile_work(): pl.pallas_call(tile_kernel, out_shape=(jax.ShapeDtypeStruct(pair.shape, h...]
    dot_general x10 -> x0, matrix products: 39.6 us -> none  [the longest x1 7.2 us: body(): jnp.dot(grad_logit, w_gate.T, preferred_element_type=jnp.float32)]
    all_to_all x0 -> x2, blocking collectives: none -> 25.6 us  [the longest x1 13.4 us: body(): lax.all_to_all(left_edges.reshape(k_local, row_count, row_part, hidden_w)...]
    convert_element_type x6 -> x1, other arithmetic: 20 us -> 1.75 us  [body(): right_edges = (right_sig * right_proj).astype(jnp.bfloat16)]
    all_to_all x2 -> x0, waiting for transfers between devices: 13.2 us -> none  [the longest x1 9.82 us: body(): lax.all_to_all(left_edges.reshape(k_local, row_count, row_part, hidden_w)...]
    reduce_scatter x2, waiting for transfers between devices: 50.2 us -> 62.9 us  [the longest x1 42.2 us: body(): lax.psum_scatter(routed, 'col', scatter_dimension=0, tiled=True)]
    select_n x2 -> x0, local copies, waits for them, and re-layouts: 12.6 us -> none  [body(): chosen = jnp.take(panels, row_blocks, axis=1)]
  transfers between devices with their start and end apart: 7 -> 4, of which waited for: 7 -> 4; matrix products, arithmetic and copies ran while one was open for 14% -> 0% of each run, Pallas kernels for 0% -> 0%
where the time goes in v1:
time: 235 us
  waiting for transfers between devices  123 us (52%)
  Pallas kernels  56.3 us (24%)
  blocking collectives  25.6 us (11%)
  between operations  14.6 us (6%)
  other arithmetic  6.64 us (3%)
  local copies, waits for them, and re-layouts  6.14 us (3%)
    all_gather x1, waiting for transfers between devices, body(): panels = lax.all_gather(spread, 'col')  48.3 us
    reduce_scatter x1, waiting for transfers between devices, body(): lax.psum_scatter(routed, 'col', scatter_dimension=0, tiled=True)  42.2 us
    pallas_call x1, Pallas kernels, tile_work(): pl.pallas_call(tile_kernel, out_shape=(jax.ShapeDtypeStruct(pair.shape, h...  39.6 us
    reduce_scatter x1, waiting for transfers between devices, body(): lax.psum_scatter(right_part, 'row', scatter_dimension=0, tiled=True)  20.8 us
    pallas_call x1, Pallas kernels, sum_over_devices(): pl.pallas_call(functools.partial(sum_kernel, col_count, row_count), out_s...  16.7 us
    all_to_all x1, blocking collectives, body(): lax.all_to_all(left_edges.reshape(k_local, row_count, row_part, hidden_w)...  13.4 us
    all_to_all x1, blocking collectives, body(): lax.all_to_all(column_sum.reshape(row_count, k_local, row_part, hidden_w)...  12.3 us
    all_gather x1, waiting for transfers between devices, body(): right_full = lax.all_gather(right_edges, 'row', axis=0, tiled=True)  11.5 us
  transfers between devices with their start and end apart: 4, of which 4 were waited for; matrix products, arithmetic and copies ran while one was open for 0% of the time, Pallas kernels for 0%

profile of v1, /device:TPU:0, one launch (start us, length us, event | category | flops | bytes accessed | tf_op | source)
XLA Modules:
  0.0 235.0 jit_solution(3094057773275872541)
XLA Ops:
  7.3 1.3 copy.23
  8.7 0.2 fusion.11
  8.9 0.8 fusion.23
  9.7 1.7 multiply_convert_fusion.2
  11.5 0.4 copy-done.1
  12.0 13.4 %all_to_all.24 = bf16[16,4,32,128]{3,2,0,1:T(8,128)(2,1)} all-to-all(bf16[16,4,32,128]{3,2,0,1:T(8,128)(2,1)S(1)} %copy.25), channel_id=1, replica_groups=mesh['groups'=2,'col'=4,'row'=4] {'row'}, dimensions={1} | all-to-all | bytes 1048576 | tf_op jit(solution)/shard_map/all_to_all | solution.py:297
  26.1 11.5 %all-gather.5.cloned.1.call-done.right_ref = bf16[64,128,128]{2,1,0:T(8,128)(2,1)} async-done(((bf16[16,128,128]{2,1,0:T(8,128)(2,1)}), bf16[64,128,128]{2,1,0:T(8,128)(2,1)}) %all-gather.5.cloned.1.call-update) | async-done | bytes 2097168 | tf_op jit(solution)/shard_map/all_gather | solution.py:305
  37.6 48.3 %all-gather.3.cloned.1.call-done = bf16[4,64,1,32,128]{4,3,2,1,0:T(8,128)(2,1)} async-done(((bf16[1,64,1,32,128]{4,3,2,1,0:T(8,128)(2,1)}), bf16[4,64,1,32,128]{4,3,2,1,0:T(8,128)(2,1)}) %all-gather.3.cloned.1.call-update) | async-done | bytes 2097168 | tf_op jit(solution)/shard_map/all_gather | solution.py:304
  85.9 39.6 %tile_work.1 = (bf16[2,32,128,128]{3,2,1,0:T(8,128)(2,1)}, bf16[2,32,128,128]{3,2,1,0:T(8,128)(2,1)}, bf16[4,64,32,128]{3,2,1,0:T(8,128)(2,1)}, bf16[64,128,128]...) custom-call(s32[1,2]{1,0:T(1,128)} %rows_ref.1, s32[1]{0:T(128)S(6)} %copy.30.count_ref, ...), custom_call_target="tpu_custom_call" | custom-call | tf_op jit(solution)/shard_map/tile_work/pallas_call | solution.py:148
  125.6 0.5 reduce-scatter.5.cloned.1.call-update
  126.1 42.2 %reduce-scatter.3.cloned.1.call-done = bf16[1,64,32,128]{3,2,1,0:T(8,128)(2,1)} async-done(((bf16[4,64,32,128]{3,2,1,0:T(8,128)(2,1)}), bf16[1,64,32,128]{3,2,1,0:T(8,128)(2,1)}) %reduce-scatter.3.cloned.1.call-update) | async-done | bytes 524304 | tf_op jit(solution)/shard_map/reduce_scatter | solution.py:317
  168.3 12.3 %all_to_all.25 = bf16[4,16,32,128]{3,2,1,0:T(8,128)(2,1)S(1)} all-to-all(bf16[4,16,32,128]{3,2,1,0:T(8,128)(2,1)} %bitcast.44), channel_id=1, replica_groups=mesh['groups'=2,'col'=4,'row'=4] {'row'}, dimensions={0} | all-to-all | bytes 1048576 | tf_op jit(solution)/shard_map/all_to_all | solution.py:320
  180.5 0.1 convert_bitcast_fusion
  180.8 20.8 %reduce-scatter.5.cloned.1.call-done = bf16[16,128,128]{2,1,0:T(8,128)(2,1)} async-done(((bf16[64,128,128]{2,1,0:T(8,128)(2,1)}), bf16[16,128,128]{2,1,0:T(8,128)(2,1)}) %reduce-scatter.5.cloned.1.call-update) | async-done | bytes 524304 | tf_op jit(solution)/shard_map/reduce_scatter | solution.py:328
  201.5 3.4 %multiply_convert_fusion.1 = (bf16[16,128,128]{2,1,0:T(8,128)(2,1)S(1)}, bf16[16,128,128]{2,1,0:T(8,128)(2,1)S(1)}, bf16[16,128,128]{2,1,0:T(8,128)(2,1)S(1)}, bf16[16,128,128]{2,1,0:T(8,128)(2,1)S(1)}) fusion(f32[16,128,128]{2,1,0:T(8,128)S(1)} %bitcast.35, f32[16,128,512]{2,1,0:T(8,128)} %copy-done.1, bf16[16,128,128]{2,1,0:T(8,128)(2,1)} %reduce-scatter.5.cloned.1.call-done), kind=kLoop, calls=%fused_computation.33 | loop fusion | flops 5505024 | bytes 7864320 | tf_op jit(solution)/shard_map/convert.3
  205.0 0.5 convolution_bitcast_fusion
  205.5 0.8 fusion.29
  206.4 0.8 pad_maximum_fusion.1
  207.2 16.7 %sum_over_devices.1 = f32[16,48,128]{2,1,0:T(8,128)} custom-call(f32[16,48,128]{2,1,0:T(8,128)} %bitcast.43), custom_call_target="tpu_custom_call" | custom-call | tf_op jit(solution)/shard_map/sum_over_devices/pallas_call | solution.py:249
  223.9 1.5 fusion.30
  225.4 1.0 slice.32
  226.4 0.3 fusion.10
  226.7 1.0 copy.28
  227.7 0.7 reshape.96
  (29 shorter events, 0.5 us)
Async XLA Ops:
  7.2 1.7 copy-start
  7.2 1.7 copy-start.6
  7.2 1.7 copy-start.4
  7.2 30.4 %all-gather.5.cloned.1.call-start = ((), (), s32[]{:S(2)}) async-start(), calls=%async_computation.5 | async-start | bytes 2621440 | tf_op jit(solution)/shard_map/all_gather | solution.py:305
  9.7 2.1 copy-start.1
  11.9 74.0 %all-gather.3.cloned.1.call-start = ((), (), s32[]{:S(2)}) async-start(), calls=%async_computation.4 | async-start | bytes 2621440 | tf_op jit(solution)/shard_map/all_gather | solution.py:304
  25.4 142.9 %reduce-scatter.3.cloned.1.call-start = ((), (), s32[]{:S(2)}) async-start(), calls=%async_computation.6 | async-start | bytes 2621440 | tf_op jit(solution)/shard_map/reduce_scatter | solution.py:317
  125.5 76.0 %reduce-scatter.5.cloned.1.call-start = ((), (), s32[]{:S(2)}) async-start(), calls=%async_computation.7 | async-start | bytes 2621440 | tf_op jit(solution)/shard_map/reduce_scatter | solution.py:328
  201.5 3.4 %copy-start.5 = (f32[128]{0:T(128)S(1)}, f32[128]{0:T(128)}, u32[]{:S(2)}) copy-start(f32[128]{0:T(128)} %param.18) | copy-start | bytes 1540
  201.5 3.4 %copy-start.7 = (f32[128]{0:T(128)S(1)}, f32[128]{0:T(128)}, u32[]{:S(2)}) copy-start(f32[128]{0:T(128)} %param.17) | copy-start | bytes 1540
  205.5 0.9 copy-start.2
  205.5 0.9 copy-start.3
Sparse Core Ops, SparseCore 0:
  12.0 25.5 all-gather.4
  39.2 46.6 all-gather.2
  125.6 42.5 reduce-scatter.2
  170.8 30.6 reduce-scatter.4

commit v2 on v1

--- a/solution.py
+++ b/solution.py
@@ -262,6 +262,119 @@
     )(grads)
 
 
+def exchange_kernel(
+    forward,
+    col_count,
+    row_count,
+    left_ref,
+    right_ref,
+    left_out,
+    right_out,
+    left_sems,
+    right_sems,
+):
+    group, col, row = lax.axis_index("groups"), lax.axis_index("col"), lax.axis_index("row")
+    count = col_count * row_count
+    me = col * row_count + row
+    if forward:
+        depth, part = left_ref.shape[0], left_ref.shape[1] // row_count
+    else:
+        depth, part = left_ref.shape[1] // row_count, left_ref.shape[2]
+
+    def slab(index):
+        return pl.ds(pl.multiple_of(index * depth, depth), depth)
+
+    def cells(index):
+        return pl.ds(pl.multiple_of(index * part, part), part)
+
+    def left_ends(to_col, to_row):
+        if forward:
+            return left_ref.at[:, cells(to_row)], left_out.at[col, slab(row)]
+        return left_ref.at[to_col, slab(to_row)], left_out.at[col, :, cells(row)]
+
+    def right_ends(to_row):
+        if forward:
+            return right_ref, right_out.at[slab(row)]
+        return right_ref.at[slab(to_row)], right_out.at[row]
+
+    def send(ends, sems, step, to_col, to_row):
+        return pltpu.make_async_remote_copy(
+            src_ref=ends[0],
+            dst_ref=ends[1],
+            send_sem=sems.at[0, step],
+            recv_sem=sems.at[1, step],
+            device_id=(group, to_col, to_row),
+            device_id_type=pl.DeviceIdType.MESH,
+        )
+
+    def left_copy(step):
+        to = (me + step) % count
+        to_col, to_row = to // row_count, to % row_count
+        return send(left_ends(to_col, to_row), left_sems, step, to_col, to_row)
+
+    def right_copy(step):
+        to_row = (row + step) % row_count
+        return send(right_ends(to_row), right_sems, step, col, to_row)
+
+    barrier = pltpu.get_barrier_semaphore()
+
+    @pl.loop(1, count)
+    def _(step):
+        to = (me + step) % count
+        pl.semaphore_signal(
+            barrier,
+            inc=1,
+            device_id=(group, to // row_count, to % row_count),
+            device_id_type=pl.DeviceIdType.MESH,
+        )
+
+    own_left = pltpu.make_async_copy(*left_ends(col, row), left_sems.at[0, 0])
+    own_right = pltpu.make_async_copy(*right_ends(row), right_sems.at[0, 0])
+    own_left.start()
+    own_right.start()
+    pl.semaphore_wait(barrier, count - 1)
+
+    @pl.loop(1, count)
+    def _(step):
+        left_copy(step).start()
+
+    @pl.loop(1, row_count)
+    def _(step):
+        right_copy(step).start()
+
+    own_left.wait()
+    own_right.wait()
+
+    @pl.loop(1, count)
+    def _(step):
+        left_copy(step).wait()
+
+    @pl.loop(1, row_count)
+    def _(step):
+        right_copy(step).wait()
+
+
+def exchange(forward, left, right, left_shape, right_shape, col_count, row_count):
+    anywhere = pl.BlockSpec(memory_space=pl.ANY)
+    return pl.pallas_call(
+        functools.partial(exchange_kernel, forward, col_count, row_count),
+        out_shape=(
+            jax.ShapeDtypeStruct(left_shape, left.dtype),
+            jax.ShapeDtypeStruct(right_shape, right.dtype),
+        ),
+        in_specs=[anywhere, anywhere],
+        out_specs=(anywhere, anywhere),
+        scratch_shapes=[
+            pltpu.SemaphoreType.DMA((2, col_count * row_count)),
+            pltpu.SemaphoreType.DMA((2, row_count)),
+        ],
+        compiler_params=pltpu.CompilerParams(
+            collective_id=1 if forward else 2, has_side_effects=True
+        ),
+        name="gather_edges" if forward else "scatter_terms",
+    )(left, right)
+
+
 def body(
     pair_slab,
     tile_pair,
@@ -294,19 +407,20 @@
     right_sig = jax.nn.sigmoid(project[..., 3 * hidden_w :])
     left_edges = (left_sig * left_proj).astype(jnp.bfloat16)
     right_edges = (right_sig * right_proj).astype(jnp.bfloat16)
-    spread = lax.all_to_all(
-        left_edges.reshape(k_local, row_count, row_part, hidden_w),
-        "row",
-        split_axis=1,
-        concat_axis=0,
-        tiled=True,
-    )
-    panels = lax.all_gather(spread, "col")
-    right_full = lax.all_gather(right_edges, "row", axis=0, tiled=True)
+    depth = k_local * row_count
+    panels, right_full = exchange(
+        True,
+        left_edges,
+        right_edges,
+        (col_count, depth, row_part, hidden_w),
+        (depth, tile_len, hidden_w),
+        col_count,
+        row_count,
+    )
     update, pair_back, routed, right_part, out_total, gate_total = tile_work(
         tile_rows,
         tile_count,
-        panels.reshape(col_count, -1, row_part, hidden_w),
+        panels,
         right_full,
         tile_pair[0],
         tile_cotan[0],
@@ -314,20 +428,17 @@
         w_out,
         w_gate,
     )
-    column_sum = lax.psum_scatter(
-        routed, "col", scatter_dimension=0, tiled=True
-    ).astype(jnp.float32)
-    returned = lax.all_to_all(
-        column_sum.reshape(row_count, k_local, row_part, hidden_w).astype(jnp.bfloat16),
-        "row",
-        split_axis=0,
-        concat_axis=2,
-        tiled=True,
-    ).astype(jnp.float32)
-    left_grad = returned.reshape(k_local, tile_len, hidden_w)
-    right_grad = lax.psum_scatter(
-        right_part, "row", scatter_dimension=0, tiled=True
-    ).astype(jnp.float32)
+    left_terms, right_terms = exchange(
+        False,
+        routed,
+        right_part,
+        (col_count, k_local, tile_len, hidden_w),
+        (row_count, k_local, tile_len, hidden_w),
+        col_count,
+        row_count,
+    )
+    left_grad = jnp.sum(left_terms.astype(jnp.float32), axis=0)
+    right_grad = jnp.sum(right_terms.astype(jnp.float32), axis=0)
     grad_project = jnp.concatenate(
         [
             left_grad * left_sig,

time: 235 us -> 175 us (0.74)
  waiting for transfers between devices: 123 us -> 0 us
  Pallas kernels: 56.3 us -> 159 us
  blocking collectives: 25.6 us -> 0 us
  between operations: 14.6 us -> 1.56 us
    pallas_call x0 -> x2, Pallas kernels: none -> 102 us  [exchange(): pl.pallas_call(functools.partial(exchange_kernel, forward, col_count, row...]
    reduce_scatter x2 -> x0, waiting for transfers between devices: 62.9 us -> none  [the longest x1 42.2 us: body(): lax.psum_scatter(routed, 'col', scatter_dimension=0, tiled=True)]
    all_gather x2 -> x0, waiting for transfers between devices: 59.8 us -> none  [the longest x1 48.3 us: body(): panels = lax.all_gather(spread, 'col')]
    all_to_all x2 -> x0, blocking collectives: 25.6 us -> none  [the longest x1 13.4 us: body(): lax.all_to_all(left_edges.reshape(k_local, row_count, row_part, hidden_w)...]
    reduce_sum x0 -> x1, other arithmetic: none -> 3.37 us  [body(): right_grad = jnp.sum(right_terms.astype(jnp.float32), axis=0)]
    another operation x1, other arithmetic: 3.42 us -> 1 us
  transfers between devices with their start and end apart: 4 -> 0, of which waited for: 4 -> 0; matrix products, arithmetic and copies ran while one was open for 0% -> 0% of each run, Pallas kernels for 0% -> 0%
where the time goes in v2:
time: 175 us
  Pallas kernels  159 us (91%)
  other arithmetic  7.64 us (4%)
  local copies, waits for them, and re-layouts  4.24 us (2%)
  matrix products  2.15 us (1%)
    pallas_call x2, Pallas kernels, exchange(): pl.pallas_call(functools.partial(exchange_kernel, forward, col_count, row...  102 us
    pallas_call x1, Pallas kernels, tile_work(): pl.pallas_call(tile_kernel, out_shape=(jax.ShapeDtypeStruct(pair.shape, h...  39.6 us
    pallas_call x1, Pallas kernels, sum_over_devices(): pl.pallas_call(functools.partial(sum_kernel, col_count, row_count), out_s...  17.4 us

profile of v2, /device:TPU:0, one launch (start us, length us, event | category | flops | bytes accessed | tf_op | source)
XLA Modules:
  0.0 174.7 jit_solution(358696559805290201)
XLA Ops:
  0.6 0.0 copy-start
  0.6 0.0 copy-start.8
  0.7 0.0 copy-start.6
  1.4 1.3 copy.18
  2.7 0.1 convert_reduce_fusion.2
  2.8 0.2 fusion.11
  3.0 0.8 fusion.19
  3.8 1.9 %multiply_convert_fusion.4 = (bf16[16,128,128]{2,1,0:T(8,128)(2,1)}, bf16[16,128,128]{2,1,0:T(8,128)(2,1)}) fusion(f32[16,128,512]{2,1,0:T(8,128)S(1)} %fusion.19), kind=kLoop, calls=%fused_computation.31 | loop fusion | flops 2621440 | bytes 5242880 | tf_op jit(solution)/shard_map/convert_element_type | solution.py:409
  5.7 0.4 copy-done.1
  6.1 52.1 %gather_edges.1 = (bf16[4,64,32,128]{3,2,1,0:T(8,128)(2,1)}, bf16[64,128,128]{2,1,0:T(8,128)(2,1)}) custom-call(bf16[16,128,128]{2,1,0:T(8,128)(2,1)} %get-tuple-element.41.left_ref, bf16[16,128,128]{2,1,0:T(8,128)(2,1)} %get-tuple-element.40.right_ref), custom_call_target="tpu_custom_call" | custom-call | tf_op jit(solution)/shard_map/gather_edges/pallas_call | solution.py:359
  58.3 39.6 %tile_work.1 = (bf16[2,32,128,128]{3,2,1,0:T(8,128)(2,1)}, bf16[2,32,128,128]{3,2,1,0:T(8,128)(2,1)}, bf16[4,64,32,128]{3,2,1,0:T(8,128)(2,1)}, bf16[64,128,128]...) custom-call(s32[1,2]{1,0:T(1,128)} %rows_ref.1, s32[1]{0:T(128)S(6)} %copy.22.count_ref, ...), custom_call_target="tpu_custom_call" | custom-call | tf_op jit(solution)/shard_map/tile_work/pallas_call | solution.py:148
  97.8 50.0 %scatter_terms.1 = (bf16[4,16,128,128]{3,2,1,0:T(8,128)(2,1)}, bf16[4,16,128,128]{3,2,1,0:T(8,128)(2,1)}) custom-call(bf16[4,64,32,128]{3,2,1,0:T(8,128)(2,1)} %get-tuple-element.19.left_ref, bf16[64,128,128]{2,1,0:T(8,128)(2,1)} %get-tuple-element.20.right_ref), custom_call_target="tpu_custom_call" | custom-call | tf_op jit(solution)/shard_map/scatter_terms/pallas_call | solution.py:359
  147.8 3.4 %convert_reduce_fusion = (f32[16,128,128]{2,1,0:T(8,128)S(1)}, f32[16,128,128]{2,1,0:T(8,128)S(1)}) fusion(bf16[4,16,128,128]{3,2,1,0:T(8,128)(2,1)} %get-tuple-element.22, bf16[4,16,128,128]{3,2,1,0:T(8,128)(2,1)} %get-tuple-element.21), kind=kLoop, calls=%fused_computation | loop fusion | flops 3670016 | bytes 6291456 | tf_op jit(solution)/shard_map/reduce_sum | solution.py:441
  151.2 0.1 copy-done.2
  151.3 1.0 multiply_convert_fusion.3
  152.3 0.5 convolution_bitcast_fusion
  152.8 0.0 copy-start.4
  152.8 0.8 fusion.25
  153.7 0.8 pad_maximum_fusion.1
  154.5 17.4 %sum_over_devices.1 = f32[16,48,128]{2,1,0:T(8,128)} custom-call(f32[16,48,128]{2,1,0:T(8,128)} %bitcast.23), custom_call_target="tpu_custom_call" | custom-call | tf_op jit(solution)/shard_map/sum_over_devices/pallas_call | solution.py:249
  172.0 0.3 fusion.10
  172.3 1.0 copy.20
  173.3 0.7 fusion.26
  174.0 0.7 reshape.76
  (20 shorter events, 0.1 us)
Async XLA Ops:
  0.6 2.3 %copy-start = (bf16[128,512]{1,0:T(8,128)(2,1)S(1)}, bf16[128,512]{1,0:T(8,128)(2,1)}, u32[]{:S(2)}) copy-start(bf16[128,512]{1,0:T(8,128)(2,1)} %param.19) | copy-start | bytes 393220
  0.6 2.3 %copy-start.8 = (f32[128]{0:T(128)S(1)}, f32[128]{0:T(128)}, u32[]{:S(2)}) copy-start(f32[128]{0:T(128)} %param.17) | copy-start | bytes 1540
  0.7 2.3 %copy-start.6 = (f32[128]{0:T(128)S(1)}, f32[128]{0:T(128)}, u32[]{:S(2)}) copy-start(f32[128]{0:T(128)} %param.18) | copy-start | bytes 1540
  3.8 2.3 %copy-start.1 = (f32[16,128,512]{2,1,0:T(8,128)}, f32[16,128,512]{2,1,0:T(8,128)S(1)}, u32[]{:S(2)}) copy-start(f32[16,128,512]{2,1,0:T(8,128)S(1)} %fusion.19) | copy-start | bytes 12582916
  147.8 3.5 %copy-start.2 = (f32[16,128,512]{2,1,0:T(8,128)S(1)}, f32[16,128,512]{2,1,0:T(8,128)}, u32[]{:S(2)}) copy-start(f32[16,128,512]{2,1,0:T(8,128)} %copy-done.1) | copy-start | bytes 12582916
  151.3 1.0 copy-start.7
  151.3 1.0 copy-start.9
  152.8 0.9 copy-start.4
  152.8 0.9 copy-start.5
  171.9 1.4 copy-start.3

commit v3 on v2

--- a/solution.py
+++ b/solution.py
@@ -84,7 +84,7 @@
         for column in range(left_ref.shape[0]):
             left_ref[column, at] = jnp.zeros((chunk,) + left_ref.shape[2:], left_ref.dtype)
 
-    @pl.loop(0, hidden, unroll=4)
+    @pl.loop(0, hidden, unroll=16)
     def _(h):
         comb_major[h] = dot(left_major[h], right_major[h], 0, 0)
 
@@ -120,7 +120,7 @@
             comb_back = comb_back.reshape(chunk, tile_len, hidden)
             back_major[:, at_all, :] = to_hidden_major(comb_back).astype(jnp.bfloat16)
 
-    @pl.loop(0, hidden, unroll=4)
+    @pl.loop(0, hidden, unroll=16)
     def _(h):
         back = back_major[h]
         right_back[h] = dot(left_major[h], back, 1, 0).astype(jnp.bfloat16)

time: 175 us -> 168 us (0.960)
  Pallas kernels: 159 us -> 152 us
    pallas_call x1, Pallas kernels: 39.6 us -> 32.4 us  [tile_work(): pl.pallas_call(tile_kernel, out_shape=(jax.ShapeDtypeStruct(pair.shape, h...]
where the time goes in v3:
time: 168 us
  Pallas kernels  152 us (90%)
  other arithmetic  7.64 us (5%)
  local copies, waits for them, and re-layouts  4.24 us (3%)
  matrix products  2.14 us (1%)
    pallas_call x2, Pallas kernels, exchange(): pl.pallas_call(functools.partial(exchange_kernel, forward, col_count, row...  102 us
    pallas_call x1, Pallas kernels, tile_work(): pl.pallas_call(tile_kernel, out_shape=(jax.ShapeDtypeStruct(pair.shape, h...  32.4 us
    pallas_call x1, Pallas kernels, sum_over_devices(): pl.pallas_call(functools.partial(sum_kernel, col_count, row_count), out_s...  17.4 us
    reduce_sum x1, other arithmetic, body(): right_grad = jnp.sum(right_terms.astype(jnp.float32), axis=0)  3.37 us

profile of v3, /device:TPU:0, one launch (start us, length us, event | category | flops | bytes accessed | tf_op | source)
XLA Modules:
  0.0 167.5 jit_solution(17814949889507009194)
XLA Ops:
  0.6 0.0 copy-start
  0.6 0.0 copy-start.8
  0.7 0.0 copy-start.6
  1.4 1.3 copy.18
  2.7 0.1 convert_reduce_fusion.2
  2.8 0.2 fusion.11
  3.0 0.8 fusion.19
  3.8 1.9 %multiply_convert_fusion.4 = (bf16[16,128,128]{2,1,0:T(8,128)(2,1)}, bf16[16,128,128]{2,1,0:T(8,128)(2,1)}) fusion(f32[16,128,512]{2,1,0:T(8,128)S(1)} %fusion.19), kind=kLoop, calls=%fused_computation.31 | loop fusion | flops 2621440 | bytes 5242880 | tf_op jit(solution)/shard_map/convert_element_type | solution.py:409
  5.7 0.4 copy-done.1
  6.1 52.1 %gather_edges.1 = (bf16[4,64,32,128]{3,2,1,0:T(8,128)(2,1)}, bf16[64,128,128]{2,1,0:T(8,128)(2,1)}) custom-call(bf16[16,128,128]{2,1,0:T(8,128)(2,1)} %get-tuple-element.41.left_ref, bf16[16,128,128]{2,1,0:T(8,128)(2,1)} %get-tuple-element.40.right_ref), custom_call_target="tpu_custom_call" | custom-call | tf_op jit(solution)/shard_map/gather_edges/pallas_call | solution.py:359
  58.3 32.4 %tile_work.1 = (bf16[2,32,128,128]{3,2,1,0:T(8,128)(2,1)}, bf16[2,32,128,128]{3,2,1,0:T(8,128)(2,1)}, bf16[4,64,32,128]{3,2,1,0:T(8,128)(2,1)}, bf16[64,128,128]...) custom-call(s32[1,2]{1,0:T(1,128)} %rows_ref.1, s32[1]{0:T(128)S(6)} %copy.22.count_ref, ...), custom_call_target="tpu_custom_call" | custom-call | tf_op jit(solution)/shard_map/tile_work/pallas_call | solution.py:148
  90.6 50.0 %scatter_terms.1 = (bf16[4,16,128,128]{3,2,1,0:T(8,128)(2,1)}, bf16[4,16,128,128]{3,2,1,0:T(8,128)(2,1)}) custom-call(bf16[4,64,32,128]{3,2,1,0:T(8,128)(2,1)} %get-tuple-element.19.left_ref, bf16[64,128,128]{2,1,0:T(8,128)(2,1)} %get-tuple-element.20.right_ref), custom_call_target="tpu_custom_call" | custom-call | tf_op jit(solution)/shard_map/scatter_terms/pallas_call | solution.py:359
  140.6 3.4 %convert_reduce_fusion = (f32[16,128,128]{2,1,0:T(8,128)S(1)}, f32[16,128,128]{2,1,0:T(8,128)S(1)}) fusion(bf16[4,16,128,128]{3,2,1,0:T(8,128)(2,1)} %get-tuple-element.22, bf16[4,16,128,128]{3,2,1,0:T(8,128)(2,1)} %get-tuple-element.21), kind=kLoop, calls=%fused_computation | loop fusion | flops 3670016 | bytes 6291456 | tf_op jit(solution)/shard_map/reduce_sum | solution.py:441
  144.0 0.1 copy-done.2
  144.1 1.0 multiply_convert_fusion.3
  145.1 0.5 convolution_bitcast_fusion
  145.6 0.0 copy-start.4
  145.6 0.8 fusion.25
  146.5 0.8 pad_maximum_fusion.1
  147.3 17.4 %sum_over_devices.1 = f32[16,48,128]{2,1,0:T(8,128)} custom-call(f32[16,48,128]{2,1,0:T(8,128)} %bitcast.23), custom_call_target="tpu_custom_call" | custom-call | tf_op jit(solution)/shard_map/sum_over_devices/pallas_call | solution.py:249
  164.8 0.3 fusion.10
  165.1 1.0 copy.20
  166.1 0.7 fusion.26
  166.8 0.7 reshape.76
  (20 shorter events, 0.1 us)
Async XLA Ops:
  0.6 2.3 %copy-start = (bf16[128,512]{1,0:T(8,128)(2,1)S(1)}, bf16[128,512]{1,0:T(8,128)(2,1)}, u32[]{:S(2)}) copy-start(bf16[128,512]{1,0:T(8,128)(2,1)} %param.19) | copy-start | bytes 393220
  0.6 2.3 %copy-start.8 = (f32[128]{0:T(128)S(1)}, f32[128]{0:T(128)}, u32[]{:S(2)}) copy-start(f32[128]{0:T(128)} %param.17) | copy-start | bytes 1540
  0.7 2.3 %copy-start.6 = (f32[128]{0:T(128)S(1)}, f32[128]{0:T(128)}, u32[]{:S(2)}) copy-start(f32[128]{0:T(128)} %param.18) | copy-start | bytes 1540
  3.8 2.3 %copy-start.1 = (f32[16,128,512]{2,1,0:T(8,128)}, f32[16,128,512]{2,1,0:T(8,128)S(1)}, u32[]{:S(2)}) copy-start(f32[16,128,512]{2,1,0:T(8,128)S(1)} %fusion.19) | copy-start | bytes 12582916
  140.6 3.5 %copy-start.2 = (f32[16,128,512]{2,1,0:T(8,128)S(1)}, f32[16,128,512]{2,1,0:T(8,128)}, u32[]{:S(2)}) copy-start(f32[16,128,512]{2,1,0:T(8,128)} %copy-done.1) | copy-start | bytes 12582916
  144.1 1.0 copy-start.7
  144.1 1.0 copy-start.9
  145.6 0.9 copy-start.4
  145.6 0.9 copy-start.5
  164.7 1.4 copy-start.3
